TPU v7x, 256 devices: a whole 4x4x8 slice. The times are simulated.
256 devices in a mesh: node: 16 (over y, x), local: 16 (over z, core).
Axes of the slice: x: 4, y: 4, z: 8, core: 2. Of those that a mesh axis runs over, the one named last changes fastest.
Arguments:
- frames: bfloat16 [262144, 1024], P(('node', 'local')), may hold values from -6 to 6
- lengths: int32 [256, 4], P(('node', 'local')), may hold values from 1 to 256, 768 in all within a row
- routes: int32 [262144, 2], P(('node', 'local')), may hold values from 0 to 63, all different within a row
- owners: int32 [32, 1], replicated, may hold values from 0 to 15; in each aligned block of 32 rows (0 to 31, 32 to 63, ...) at most 6 rows name the same one
- pw_weight: bfloat16 [1024, 2048], replicated, may hold values from -0.1875 to 0.1875
- dw_kernel: bfloat16 [31, 1024], replicated, may hold values from -1 to 1
- conv_grad: bfloat16 [262144, 1024], P(('node', 'local')), may hold values from -6 to 6
- hidden_grad: bfloat16 [256, 24, 4096], P(('node', 'local')), may hold values from -0.1875 to 0.1875
Outputs:
- frame_grad: bfloat16 [262144, 1024], P(('node', 'local'))
- owned_grad: float32 [96, 1024, 128], P('node', 'local')
Inputs may be any that keep to these rules, and one draw needn't show every extreme that they name: `routes`: each frame names 2 different experts. The 4 lengths of one device sum to 768, and one of them equals 256. `owners`: no node owns more than 6 blocks and some node owns exactly 6; every node owns one or more.
All inputs are finite; a program needn't handle non-finite values.
Results may differ from a plain program's by a relative error of at most 0.0049.
Values may be sent and summed in bfloat16 or wider, within the bound.
A program may use at most 128 MiB of HBM per device.

v0:
```python
import jax
import jax.numpy as jnp
from jax import lax
from jax.sharding import PartitionSpec as P

KW = 31
UTT = 4
BW = 128


def frame_valid(length_row, frame_count):
    utt_len = frame_count // UTT
    position = jnp.arange(frame_count, dtype=jnp.int32)
    utterance_of = position // utt_len
    utt_limit = jnp.sum(
        jnp.where(
            utterance_of[:, None] == jnp.arange(UTT, dtype=jnp.int32)[None, :],
            length_row[None, :],
            0,
        ),
        axis=1,
    )
    return position % utt_len < utt_limit


def depthwise_back(upstream, kernel, valid_mask):
    frame_count, model_width = upstream.shape
    half_width = (KW - 1) // 2
    utt_len = frame_count // UTT
    masked = jnp.where(valid_mask[:, None], upstream.astype(jnp.float32), 0.0)
    utterances = masked.reshape(UTT, utt_len, model_width)
    padded = jnp.pad(utterances, ((0, 0), (half_width, half_width), (0, 0)))
    kernel_f = kernel.astype(jnp.float32)
    running = jnp.zeros((UTT, utt_len, model_width), jnp.float32)
    for offset in range(KW):
        begin = 2 * half_width - offset
        running = running + kernel_f[offset] * padded[:, begin : begin + utt_len]
    return jnp.where(valid_mask[:, None], running.reshape(frame_count, model_width), 0.0)


def conv_branch(frames, pw_weight, conv_grad, dw_kernel, valid_mask):
    model_width = frames.shape[1]
    projected = jnp.dot(frames, pw_weight, preferred_element_type=jnp.float32)
    glu_value = projected[:, :model_width]
    glu_gate = projected[:, model_width:]
    conv_back = depthwise_back(conv_grad, dw_kernel, valid_mask)
    gate_sig = jax.nn.sigmoid(glu_gate)
    d_proj = jnp.concatenate(
        [conv_back * gate_sig, conv_back * glu_value * gate_sig * (1.0 - gate_sig)], axis=1
    ).astype(jnp.bfloat16)
    out = lax.dot_general(
        d_proj, pw_weight, (((1,), (1,)), ((), ())), preferred_element_type=jnp.float32
    )
    return out.astype(jnp.bfloat16)


def slot_selector(routes, valid_mask, experts_here, capacity):
    expert_ids = jnp.arange(experts_here, dtype=jnp.int32)
    routed_here = (
        jnp.any(routes[:, :, None] == expert_ids[None, None, :], axis=1) & valid_mask[:, None]
    )
    slot_order = jnp.cumsum(routed_here.astype(jnp.int32), axis=0) - 1
    slot_index = jnp.arange(capacity, dtype=jnp.int32)
    return routed_here.T[:, None, :] & (slot_order.T[:, None, :] == slot_index[None, :, None])


def sum_sources(received):
    return jnp.sum(received, axis=0)


def shards(frames, lengths, routes, owners, pw_weight, dw_kernel, conv_grad, hidden_grad):
    frame_count = frames.shape[0]
    model_width = frames.shape[1]
    experts_here, capacity, hidden_units = hidden_grad.shape
    local_count = lax.axis_size("local")
    node_count = lax.axis_size("node")
    rows_local = model_width // local_count
    valid_mask = frame_valid(lengths[0], frame_count)
    selector = slot_selector(routes, valid_mask, experts_here, capacity).astype(jnp.bfloat16)
    slot_frames = jnp.einsum(
        "est,td->esd", selector, frames, preferred_element_type=jnp.float32
    ).astype(jnp.bfloat16)
    node_slice = lax.psum_scatter(
        jnp.einsum("esd,esf->def", slot_frames, hidden_grad, preferred_element_type=jnp.float32),
        "local",
        scatter_dimension=0,
        tiled=True,
    )
    frame_grad = conv_branch(frames, pw_weight, conv_grad, dw_kernel, valid_mask)
    blocks_all = owners.shape[0]
    slot_cap = max(2, 3 * blocks_all // node_count)
    block_rows = node_slice.reshape(rows_local, blocks_all, BW)
    block_owner = owners[:, 0]
    block_ids = jnp.arange(blocks_all, dtype=jnp.int32)
    earlier = (block_owner[:, None] == block_owner[None, :]) & (
        block_ids[:, None] > block_ids[None, :]
    )
    owner_rank = jnp.sum(earlier.astype(jnp.int32), axis=1)
    target_row = block_owner * slot_cap + owner_rank
    placement = (
        jnp.arange(node_count * slot_cap, dtype=jnp.int32)[:, None] == target_row[None, :]
    ).astype(jnp.float32)
    outgoing = jnp.einsum("ri,dib->rdb", placement, block_rows, precision=lax.Precision.HIGHEST)
    outgoing = outgoing.reshape(node_count, slot_cap, rows_local, BW)
    owned_grad = sum_sources(
        lax.all_to_all(outgoing, "node", split_axis=0, concat_axis=0, tiled=True)
    )
    return (frame_grad, owned_grad)


def solution(mesh):
    in_specs = (
        P(("node", "local"), None),
        P(("node", "local"), None),
        P(("node", "local"), None),
        P(),
        P(),
        P(),
        P(("node", "local"), None),
        P(("node", "local"), None, None),
    )
    out_specs = (P(("node", "local"), None), P("node", "local", None))
    return jax.shard_map(shards, mesh=mesh, in_specs=in_specs, out_specs=out_specs, check_vma=False)
```

profile of v0, /device:TPU:32, one launch (start us, length us, event | category | flops | bytes accessed | tf_op | source)
XLA Modules:
  0.0 190.8 jit_solution(15246900693741420561)
XLA Ops:
  7.2 0.0 copy-start
  7.2 0.0 reduce-scatter.2.cloned.1.call-start
  7.2 0.9 compare_reduce_fusion
  8.1 0.7 select_reduce_fusion
  8.9 0.3 reduce-window.6
  9.1 0.2 slice_reduce_fusion
  9.3 0.2 reduce-window.9
  9.5 0.1 broadcast.191
  9.6 0.0 copy-done
  9.6 8.2 %convolution_bitcast_fusion = f32[1024,1,4096]{2,0,1:T(8,128)} fusion(bf16[1024,1024]{1,0:T(8,128)(2,1)S(1)} %copy-done, bf16[1,24,4096]{2,1,0:T(8,128)(2,1)} %param.15, s32[1024]{0:T(1024)S(1)} %fusion.91, pred[1024]{0:T(1024)(128)(4,1)S(1)} %get-tuple-element.2), kind=kOutput, calls=%fused_computation | convolution fusion | flops 251731968 | bytes 19076096 | tf_op jit(solution)/shard_map/esd,esf->def/dot_general | solution.py:84
  17.8 0.0 copy-start.4
  17.8 0.0 copy-start.2
  17.8 0.0 reduce-scatter.2.cloned.1.call-update
  17.9 0.6 copy-done.4
  18.5 0.2 convert_reduce_fusion
  18.7 0.0 copy-done.2
  18.7 0.1 fusion.101
  18.8 1.9 %convert_select_fusion = f32[1024,1024]{1,0:T(8,128)S(1)} fusion(bf16[1024,1024]{1,0:T(8,128)(2,1)} %param.14, pred[1024]{0:T(1024)(128)(4,1)S(1)} %get-tuple-element.3), kind=kLoop, calls=%fused_computation.105 | loop fusion | flops 2097152 | bytes 6292480 | tf_op jit(solution)/shard_map/jit(_where)/select_n | solution.py:30
  20.7 16.9 %fusion.53 = f32[4,256,1024]{2,1,0:T(8,128)} fusion(f32[4,256,1024]{2,1,0:T(8,128)S(1)} %bitcast.82, f32[1024]{0:T(1024)S(1)} %bitcast.96, f32[1024]{0:T(1024)S(1)} %bitcast.95, f32[1024]{0:T(1024)S(1)} %bitcast.94, f32[1024]{0:T(1024)S(1)} %bitcast.93, f32[1024]{0:T(1024)S(1)} %bitcast.92, f32[1024]{0:T(1024)S(1)} %bitcast.91, f32[1024]{0:T(1024)S(1)} %bitcast.90, ...), kind=kLoop, calls=%fused_computation.84 | loop fusion | flops 63963136 | bytes 8515584 | tf_op jit(solution)/shard_map/add | solution.py:37
  37.6 80.4 %reduce-scatter.2.cloned.1.call-done = f32[64,1,4096]{2,0,1:T(8,128)} async-done(((f32[1024,1,4096]{2,0,1:T(8,128)}), f32[64,1,4096]{2,0,1:T(8,128)}) %reduce-scatter.2.cloned.1.call-update) | async-done | bytes 1048592 | tf_op jit(solution)/shard_map/reduce_scatter | solution.py:83
  118.1 1.4 copy.13
  119.5 1.4 fusion.79
  120.9 2.7 %copy.11 = f32[16,6,64,128]{3,2,1,0:T(8,128)} copy(f32[16,6,64,128]{3,0,2,1:T(8,128)S(1)} %fusion.79) | data formatting | bytes 6291456 | tf_op jit(solution)/shard_map/ri,dib->rdb/dot_general | solution.py:103
  123.6 7.1 %all-to-all-start = ((f32[16,6,64,128]{3,2,1,0:T(8,128)}), f32[16,6,64,128]{3,2,1,0:T(8,128)}, u32[]{:S(2)}, u32[]{:S(2)}) async-start(f32[16,6,64,128]{3,2,1,0:T(8,128)} %copy.11), calls=%async_computation.1 | async-start | bytes 6291456 | tf_op jit(solution)/shard_map/all_to_all | solution.py:106
  130.7 0.0 copy-start.1
  130.7 6.4 %fusion.103 = f32[1024,2048]{1,0:T(8,128)S(1)} fusion(bf16[1024,1024]{1,0:T(8,128)(2,1)S(1)} %copy-done, bf16[1024,2048]{1,0:T(8,128)(2,1)} %param.12), kind=kOutput, calls=%fused_computation.152 | convolution fusion | flops 4294967296 | bytes 14680064 | tf_op jit(solution)/shard_map/dot_general | solution.py:43
  137.2 0.0 copy-done.1
  137.2 0.0 copy-start.3
  137.2 2.8 %multiply_convert_fusion = (bf16[1024,1024]{1,0:T(8,128)(2,1)S(1)}, bf16[1024,1024]{1,0:T(8,128)(2,1)S(1)}) fusion(f32[4,256,1024]{2,1,0:T(8,128)S(1)} %copy-done.1, pred[1024]{0:T(1024)(128)(4,1)S(1)} %get-tuple-element.3, f32[1024,2048]{1,0:T(8,128)S(1)} %fusion.103), kind=kLoop, calls=%fused_computation.104 | loop fusion | flops 11534336 | bytes 16778240 | tf_op jit(solution)/shard_map/convert
  140.0 0.0 copy-done.3
  140.0 5.7 %fusion.70 = bf16[1024,1024]{1,0:T(8,128)(2,1)} fusion(bf16[1024,2048]{1,0:T(8,128)(2,1)S(1)} %copy-done.3, bf16[1024,1024]{1,0:T(8,128)(2,1)S(1)} %get-tuple-element.5, bf16[1024,1024]{1,0:T(8,128)(2,1)S(1)} %get-tuple-element.4), kind=kOutput, calls=%fused_computation.106 | convolution fusion | flops 4304404480 | bytes 10485760 | tf_op jit(solution)/shard_map/dot_general | solution.py:51
  145.7 35.5 %all-to-all-done = f32[16,6,64,128]{3,2,1,0:T(8,128)} async-done(((f32[16,6,64,128]{3,2,1,0:T(8,128)}), f32[16,6,64,128]{3,2,1,0:T(8,128)}, u32[]{:S(2)}, u32[]{:S(2)}) %all-to-all-start) | async-done | bytes 3145760 | tf_op jit(solution)/shard_map/all_to_all | solution.py:106
  181.2 2.8 %reduce_sum.32 = f32[6,64,128]{2,1,0:T(8,128)} reduce(f32[16,6,64,128]{3,2,1,0:T(8,128)} %all-to-all-done, f32[]{:T(128)} %constant.50.clone.1), dimensions={0}, to_apply=%region_6.7 | reduce | flops 737280 | bytes 3342340 | tf_op jit(solution)/shard_map/reduce_sum | solution.py:68
  (8 shorter events, 0.1 us)
Async XLA Ops:
  7.2 2.4 %copy-start = (bf16[1024,1024]{1,0:T(8,128)(2,1)S(1)}, bf16[1024,1024]{1,0:T(8,128)(2,1)}, u32[]{:S(2)}) copy-start(bf16[1024,1024]{1,0:T(8,128)(2,1)} %param.8) | copy-start | bytes 6291460
  7.2 110.9 %reduce-scatter.2.cloned.1.call-start = ((), (), s32[]{:S(2)}) async-start(), calls=%async_computation.2 | async-start | bytes 17825792 | tf_op jit(solution)/shard_map/reduce_scatter | solution.py:83
  17.8 0.7 copy-start.4
  17.8 0.9 copy-start.2
  123.6 57.6 %all-to-all-start = ((f32[16,6,64,128]{3,2,1,0:T(8,128)}), f32[16,6,64,128]{3,2,1,0:T(8,128)}, u32[]{:S(2)}, u32[]{:S(2)}) async-start(f32[16,6,64,128]{3,2,1,0:T(8,128)} %copy.11), calls=%async_computation.1 | async-start | bytes 6291456 | tf_op jit(solution)/shard_map/all_to_all | solution.py:106
  130.7 6.5 %copy-start.1 = (f32[4,256,1024]{2,1,0:T(8,128)S(1)}, f32[4,256,1024]{2,1,0:T(8,128)}, u32[]{:S(2)}) copy-start(f32[4,256,1024]{2,1,0:T(8,128)} %fusion.53) | copy-start | bytes 12582916
  137.2 2.8 %copy-start.3 = (bf16[1024,2048]{1,0:T(8,128)(2,1)S(1)}, bf16[1024,2048]{1,0:T(8,128)(2,1)}, u32[]{:S(2)}) copy-start(bf16[1024,2048]{1,0:T(8,128)(2,1)} %param.12) | copy-start | bytes 12582916
Sparse Core Ops, SparseCore 0:
  18.0 100.0 reduce-scatter.1
where the time goes:
time: 191 us
  waiting for transfers between devices  116 us (61%)
  other arithmetic  26.7 us (14%)
  matrix products  21.8 us (11%)
  between operations  14.2 us (7%)
  starting transfers between devices  7.13 us (4%)
  local copies, waits for them, and re-layouts  5.08 us (3%)
    reduce_scatter x1, waiting for transfers between devices, shards(): lax.psum_scatter(jnp.einsum('esd,esf->def', slot_frames, hidden_grad, pre...  80.4 us
    all_to_all x1, waiting for transfers between devices, shards(): lax.all_to_all(outgoing, 'node', split_axis=0, concat_axis=0, tiled=True)  35.5 us
    add x1, other arithmetic, depthwise_back(): running = running + kernel_f[offset] * padded[:, begin:begin + utt_len]  16.9 us
    dot_general x1, matrix products, shards(): jnp.einsum('esd,esf->def', slot_frames, hidden_grad, preferred_element_ty...  8.22 us
    all_to_all x1, starting transfers between devices, shards(): lax.all_to_all(outgoing, 'node', split_axis=0, concat_axis=0, tiled=True)  7.09 us
    dot_general x1, matrix products, conv_branch(): projected = jnp.dot(frames, pw_weight, preferred_element_type=jnp.float32)  6.44 us
    dot_general x1, matrix products, conv_branch(): lax.dot_general(d_proj, pw_weight, (((1,), (1,)), ((), ())), preferred_el...  5.73 us
  transfers between devices with their start and end apart: 2, of which 2 were waited for; matrix products, arithmetic and copies ran while one was open for 18% of the time, Pallas kernels for 0%

commit v1 on v0

v1 whole, which is shorter than its diff:
```python
import functools

import jax
import jax.numpy as jnp
from jax import lax
from jax.experimental import pallas as pl
from jax.experimental.pallas import tpu as pltpu
from jax.sharding import PartitionSpec as P

MESH = pl.DeviceIdType.MESH
F32, BF16, I32 = jnp.float32, jnp.bfloat16, jnp.int32

TILE = 128
UTT_LEN = 256
KW = 31
CAPR = 24
CHUNKS = 2
CAP = 6


def kernel(
    slots,
    lengths, owners, routes, frames, hidden, weight, taps_hbm, conv_grad,
    out, owned,
    frames_v, hidden_v, weight_v, taps_v, conv_v, out_v, owned_v,
    flags, glu, padded, dproj,
    send1, recv1, piece, piece_b, recv2, half_b, recv3, total_b, gathered,
    load_sem, store_sem,
    send1_sem, recv1_sem, send2_sem, recv2_sem, send3_sem, recv3_sem, send4_sem, recv4_sem,
):
    node, local = lax.axis_index("node"), lax.axis_index("local")
    z, core = local // 2, local % 2
    partner = local + 1 - 2 * core

    def loads():
        yield frames, frames_v, 0
        yield hidden.at[0], hidden_v, 1
        yield taps_hbm, taps_v, 2
        yield conv_grad, conv_v, 3
        for cb in range(8):
            for part in range(2):
                yield (
                    weight.at[:, pl.ds(part * 1024 + cb * TILE, TILE)],
                    weight_v.at[:, pl.ds(cb * 256 + part * TILE, TILE)],
                    4 + cb * 2 + part,
                )

    copies = [pltpu.make_async_copy(s, d, load_sem.at[i]) for s, d, i in loads()]
    for copy in copies:
        copy.start()

    barrier = pltpu.get_barrier_semaphore()

    def greet(o, c):
        pl.semaphore_signal(barrier, inc=1, device_id=((node + o) % 16, local), device_id_type=MESH)
        return c

    def greet_z(o, c):
        pl.semaphore_signal(
            barrier, inc=1, device_id=(node, (z + o) % 8 * 2 + core), device_id_type=MESH
        )
        return c

    lax.fori_loop(1, 16, greet, 0)
    lax.fori_loop(1, 8, greet_z, 0)
    pl.semaphore_signal(barrier, inc=1, device_id=(node, partner), device_id_type=MESH)

    lane = lax.broadcasted_iota(I32, (1, TILE), 1)
    for r in range(8):
        named = routes[:, r * TILE:(r + 1) * TILE] == 0
        named = jnp.max(named.astype(I32), axis=0, keepdims=True)
        valid = lane + (r % 2) * TILE < lengths[0, r // 2]
        flags[r:r + 1, :] = jnp.where(valid, named, 0).astype(F32)
    routed = flags[...]
    upto = (
        lax.broadcasted_iota(I32, (TILE, TILE), 0) <= lax.broadcasted_iota(I32, (TILE, TILE), 1)
    ).astype(F32)
    before = (
        lax.broadcasted_iota(I32, (8, 8), 1) < lax.broadcasted_iota(I32, (8, 8), 0)
    ).astype(F32)
    in_row = jnp.dot(routed, upto, preferred_element_type=F32)
    row_sum = jnp.broadcast_to(jnp.sum(routed, axis=1, keepdims=True), (8, TILE))
    order = in_row + jnp.dot(before, row_sum, preferred_element_type=F32)
    flags[...] = jnp.where(routed > 0, order - 1.0, -1.0)
    want = lax.broadcasted_iota(I32, (32, TILE), 0).astype(F32)
    chosen = jnp.concatenate(
        [(jnp.broadcast_to(flags[r:r + 1, :], (32, TILE)) == want).astype(F32) for r in range(8)], axis=1
    ).astype(BF16)
    copies[0].wait()
    slot = jnp.dot(chosen, frames_v[...], preferred_element_type=F32)[0:CAPR]

    group = lax.broadcasted_iota(I32, (CAPR, TILE), 1) // 32
    sets = []
    for g in range(2):
        tiles = []
        for c in range(2):
            for half in range(2):
                tile = None
                for i in range(4):
                    zz = half * 4 + i
                    part = pltpu.roll(slot[:, zz * TILE:(zz + 1) * TILE], ((i - (2 * c + g)) * 32) % TILE, 1)
                    tile = part if tile is None else jnp.where(group == i, part, tile)
                tiles.append(tile)
        sets.append(jnp.concatenate(tiles, axis=0).astype(BF16))
    copies[1].wait()
    for m in range(8):
        columns = [
            hidden_v[:, (m * 4 + t) * TILE:(m * 4 + t + 1) * TILE].astype(F32) for t in range(4)
        ]
        columns = jnp.concatenate(columns, axis=0).astype(BF16)
        for g in range(2):
            send1[g * 8 + m, 0:96, :] = sets[g]
            send1[g * 8 + m, 96:192, :] = columns
    recv1[node] = send1[node]

    pl.semaphore_wait(barrier, 23)

    rows1 = ((0, 144), (144, 48))

    def copy1(chunk, o):
        to = (node + o) % 16
        rows = pl.ds(*rows1[chunk])
        return pltpu.make_async_remote_copy(
            src_ref=send1.at[to, rows], dst_ref=recv1.at[node, rows],
            send_sem=send1_sem.at[chunk, o], recv_sem=recv1_sem.at[chunk, o],
            device_id=(to, local), device_id_type=MESH,
        )

    def copy2(chunk):
        return pltpu.make_async_remote_copy(
            src_ref=piece_b.at[chunk, 1 - core], dst_ref=recv2.at[chunk],
            send_sem=send2_sem.at[chunk], recv_sem=recv2_sem.at[chunk],
            device_id=(node, partner), device_id_type=MESH,
        )

    def copy3(chunk, o):
        to = (z + o) % 8
        return pltpu.make_async_remote_copy(
            src_ref=half_b.at[chunk, to], dst_ref=recv3.at[chunk, z],
            send_sem=send3_sem.at[chunk, o], recv_sem=recv3_sem.at[chunk, o],
            device_id=(node, to * 2 + core), device_id_type=MESH,
        )

    def copy4(chunk, o):
        to = (node + o) % 16
        return pltpu.make_async_remote_copy(
            src_ref=total_b.at[chunk], dst_ref=gathered.at[node, pl.ds(2 * chunk, 2)],
            send_sem=send4_sem.at[chunk, o], recv_sem=recv4_sem.at[chunk, o],
            device_id=(to, local), device_id_type=MESH,
        )

    def each(count, do):
        def step(o, c):
            do(o)
            return c

        lax.fori_loop(1, count, step, 0)

    for chunk in range(CHUNKS):
        each(16, lambda o: copy1(chunk, o).start())

    def multiply(chunk):
        each(16, lambda o: copy1(chunk, o).wait_recv())

        def tiles(first, count):
            rows = recv1[:, first * CAPR:(first + count) * CAPR, :].astype(F32)
            rows = rows.reshape(16, count, CAPR, TILE)
            parts = [rows[:, t].reshape(16 * CAPR, TILE) for t in range(count)]
            return jnp.concatenate(parts, axis=1).astype(BF16)

        left, right = tiles(0, 4), tiles(4 + 2 * chunk, 2)
        both = lax.dot_general(left, right, (((0,), (0,)), ((), ())), preferred_element_type=F32)
        both = both.reshape(2, 256, 256)
        piece[chunk] = both
        piece_b[chunk] = both.astype(BF16)
        copy2(chunk).start()

    def add_cores(chunk):
        copy2(chunk).wait_recv()
        half = piece[chunk, core] + recv2[chunk].astype(F32)
        half_b[chunk] = half.astype(BF16).reshape(8, 32, 256)
        recv3[chunk, z] = half_b[chunk, z]
        each(8, lambda o: copy3(chunk, o).start())

    def add_chips(chunk):
        each(8, lambda o: copy3(chunk, o).wait_recv())
        total = recv3[chunk, 0].astype(F32)
        for other in range(1, 8):
            total = total + recv3[chunk, other].astype(F32)
        total = total.astype(BF16)
        for t in range(2):
            total_b[chunk, t] = total[:, t * TILE:(t + 1) * TILE]
        for t in range(2):
            gathered[node, 2 * chunk + t] = total_b[chunk, t]
        each(16, lambda o: copy4(chunk, o).start())

    steps = {
        slots[0]: lambda: multiply(0),
        slots[1]: lambda: multiply(1),
        slots[2]: lambda: add_cores(0),
        slots[3]: lambda: add_cores(1),
        slots[4]: lambda: add_chips(0),
        slots[5]: lambda: add_chips(1),
    }

    def hook(now):
        for at, step in steps.items():
            pl.when(now == at)(step)

    padded[0:16, :] = jnp.zeros((16, TILE), F32)
    padded[272:288, :] = jnp.zeros((16, TILE), F32)
    for copy in copies[2:]:
        copy.wait()
    R = 64

    def conv_tile(u, cb):
        rows_u = pl.multiple_of(u * UTT_LEN, UTT_LEN)
        lanes = pl.ds(pl.multiple_of(cb * TILE, TILE), TILE)
        valid = lax.broadcasted_iota(I32, (UTT_LEN, TILE), 0) < lengths[0, u]
        padded[16:272, :] = jnp.where(valid, conv_v[pl.ds(rows_u, UTT_LEN), lanes].astype(F32), 0.0)
        taps = taps_v[:, lanes].astype(F32)
        for r in range(UTT_LEN // R):
            rows = pl.ds(pl.multiple_of(rows_u + r * R, R), R)
            acc = jnp.zeros((R, TILE), F32)
            for k in range(KW):
                first = r * R + KW - k
                acc = acc + taps[k:k + 1, :] * padded[first:first + R, :]
            acc = jnp.where(valid[r * R:(r + 1) * R], acc, 0.0)
            value, gate = glu[rows, 0:TILE], glu[rows, TILE:2 * TILE]
            sig = jax.nn.sigmoid(gate)
            d_value = acc * sig
            d_gate = d_value * value * (1.0 - sig)
            at = pl.multiple_of(cb * 256, 256)
            dproj[rows, pl.ds(at, TILE)] = d_value.astype(BF16)
            dproj[rows, pl.ds(at + TILE, TILE)] = d_gate.astype(BF16)

    def channels(cb, c):
        columns = pl.ds(pl.multiple_of(cb * 256, 256), 256)
        glu[...] = jnp.dot(frames_v[...], weight_v[:, columns], preferred_element_type=F32)

        def utterance(u, c):
            conv_tile(u, cb)
            hook(cb * 4 + u)
            return c

        return lax.fori_loop(0, 4, utterance, c)

    lax.fori_loop(0, 8, channels, 0)

    def store(i):
        columns = pl.ds(pl.multiple_of(i * 256, 256), 256)
        return pltpu.make_async_copy(out_v.at[:, columns], out.at[:, columns], store_sem.at[i])

    def back(i, c):
        columns = pl.ds(pl.multiple_of(i * 256, 256), 256)
        out_v[:, columns] = lax.dot_general(
            dproj[...], weight_v[columns, :], (((1,), (1,)), ((), ())), preferred_element_type=F32
        ).astype(BF16)
        store(i).start()
        hook(32 + i)
        return c

    lax.fori_loop(0, 4, back, 0)

    picks = [jnp.int32(-1)] * CAP
    held = jnp.int32(0)
    for i in range(32):
        mine = owners[i] == node
        picks = [jnp.where(mine & (held == k), i, picks[k]) for k in range(CAP)]
        held = held + mine.astype(I32)
    for chunk in range(CHUNKS):
        each(16, lambda o: copy4(chunk, o).wait_recv())
    for k in range(CAP):
        block = jnp.maximum(picks[k], 0)
        keep = jnp.broadcast_to(picks[k] >= 0, (32, TILE))
        for g in range(2):
            rows = gathered[g * 8 + block // 4, block % 4].astype(F32)
            owned_v[k, g * 32:(g + 1) * 32, :] = jnp.where(keep, rows, 0.0)
    last = pltpu.make_async_copy(owned_v, owned, load_sem.at[0])
    last.start()

    for chunk in range(CHUNKS):
        each(16, lambda o: copy1(chunk, o).wait_send())
        copy2(chunk).wait_send()
        each(8, lambda o: copy3(chunk, o).wait_send())
        each(16, lambda o: copy4(chunk, o).wait_send())
    for i in range(4):
        store(i).wait()
    last.wait()


SLOTS = (13, 17, 16, 20, 23, 28)


def shards(frames, lengths, routes, owners, pw_weight, dw_kernel, conv_grad, hidden_grad):
    smem = pl.BlockSpec(memory_space=pltpu.SMEM)
    vmem = pl.BlockSpec(memory_space=pltpu.VMEM)
    hbm = pl.BlockSpec(memory_space=pl.ANY)
    dma = pltpu.SemaphoreType.DMA
    return pl.pallas_call(
        functools.partial(kernel, SLOTS),
        out_shape=(
            jax.ShapeDtypeStruct((1024, 1024), BF16),
            jax.ShapeDtypeStruct((CAP, 64, TILE), F32),
        ),
        in_specs=[smem, smem, vmem, hbm, hbm, hbm, hbm, hbm],
        out_specs=(hbm, hbm),
        scratch_shapes=[
            pltpu.VMEM((1024, 1024), BF16),
            pltpu.VMEM((CAPR, 4096), BF16),
            pltpu.VMEM((1024, 2048), BF16),
            pltpu.VMEM((KW, 1024), BF16),
            pltpu.VMEM((1024, 1024), BF16),
            pltpu.VMEM((1024, 1024), BF16),
            pltpu.VMEM((CAP, 64, TILE), F32),
            pltpu.VMEM((8, TILE), F32),
            pltpu.VMEM((1024, 256), F32),
            pltpu.VMEM((288, TILE), F32),
            pltpu.VMEM((1024, 2048), BF16),
            pltpu.VMEM((16, 192, TILE), BF16),
            pltpu.VMEM((16, 192, TILE), BF16),
            pltpu.VMEM((CHUNKS, 2, 256, 256), F32),
            pltpu.VMEM((CHUNKS, 2, 256, 256), BF16),
            pltpu.VMEM((CHUNKS, 256, 256), BF16),
            pltpu.VMEM((CHUNKS, 8, 32, 256), BF16),
            pltpu.VMEM((CHUNKS, 8, 32, 256), BF16),
            pltpu.VMEM((CHUNKS, 2, 32, TILE), BF16),
            pltpu.VMEM((16, 4, 32, TILE), BF16),
            dma((20,)), dma((4,)),
            dma((CHUNKS, 16)), dma((CHUNKS, 16)),
            dma((CHUNKS,)), dma((CHUNKS,)),
            dma((CHUNKS, 8)), dma((CHUNKS, 8)),
            dma((CHUNKS, 16)), dma((CHUNKS, 16)),
        ],
        compiler_params=pltpu.CompilerParams(
            collective_id=0, has_side_effects=True, vmem_limit_bytes=56 * 2**20
        ),
    )(
        lengths, owners.reshape(32), routes.T, frames, hidden_grad, pw_weight, dw_kernel, conv_grad
    )


def solution(mesh):
    in_specs = (
        P(("node", "local"), None),
        P(("node", "local"), None),
        P(("node", "local"), None),
        P(),
        P(),
        P(),
        P(("node", "local"), None),
        P(("node", "local"), None, None),
    )
    out_specs = (P(("node", "local"), None), P("node", "local", None))
    return jax.shard_map(shards, mesh=mesh, in_specs=in_specs, out_specs=out_specs, check_vma=False)
```

time: 191 us -> 45.7 us (0.24)
  the two profiles are of different devices: /device:TPU:32 before, /device:TPU:4 now
where the time goes in v1:
time: 45.7 us; the launch traced here: 45.5 us
  Pallas kernels  41 us (90%)
  local copies, waits for them, and re-layouts  3.8 us (8%)
  between operations  0.65 us (1%)
    pallas_call x1, Pallas kernels, shards(): pl.pallas_call(functools.partial(kernel, SLOTS), out_shape=(jax.ShapeDtyp...  41 us
    unnamed x4, local copies, waits for them, and re-layouts  3.8 us

profile of v1, /device:TPU:4, one launch (start us, length us, event | category | flops | bytes accessed | tf_op | source)
XLA Modules:
  0.0 45.5 jit_solution(17824282498030780878)
XLA Ops:
  0.6 41.0 %shard_map.95 = (bf16[1024,1024]{1,0:T(8,128)(2,1)}, f32[6,64,128]{2,1,0:T(8,128)}) custom-call(s32[1,4]{1,0:T(1,128)} %lengths.1, s32[32]{0:T(128)} %bitcast.3, s32[2,1024]{1,0:T(2,128)} %bitcast.2, bf16[1024,1024]{1,0:T(8,128)(2,1)} %frames.1, bf16[1,24,4096]{2,1,0:T(8,128)(2,1)} %hidden.1, bf16[1024,2048]{1,0:T(8,128)(2,1)} %weight.1, ...), custom_call_target="tpu_custom_call" | custom-call | tf_op jit(solution)/shard_map/pallas_call | solution.py:300
  41.7 0.0 copy-start
  41.7 3.1 %copy.12 = bf16[1024,1024]{1,0:T(8,128)(2,1)} copy(bf16[1024,1024]{1,0:T(8,128)(2,1)} %get-tuple-element.4) | data formatting | bytes 4194304
  44.8 0.0 copy-done
  44.8 0.7 %copy.13 = f32[6,64,128]{2,1,0:T(8,128)} copy(f32[6,64,128]{2,1,0:T(8,128)S(1)} %copy-done) | data formatting | bytes 393216
Async XLA Ops:
  41.7 3.1 %copy-start = (f32[6,64,128]{2,1,0:T(8,128)S(1)}, f32[6,64,128]{2,1,0:T(8,128)}, u32[]{:S(2)}) copy-start(f32[6,64,128]{2,1,0:T(8,128)} %get-tuple-element.5) | copy-start | bytes 589828

commit v2 on v1

--- a/solution.py
+++ b/solution.py
@@ -13,6 +13,7 @@
 TILE = 128
 UTT_LEN = 256
 KW = 31
+FAR_FIRST = sorted(range(1, 16), key=lambda o: -min(o // 4, 4 - o // 4) - min(o % 4, 4 - o % 4))
 CAPR = 24
 CHUNKS = 2
 CAP = 6
@@ -20,34 +21,40 @@
 
 def kernel(
     slots,
-    lengths, owners, routes, frames, hidden, weight, taps_hbm, conv_grad,
-    out, owned,
-    frames_v, hidden_v, weight_v, taps_v, conv_v, out_v, owned_v,
-    flags, glu, padded, dproj,
-    send1, recv1, piece, piece_b, recv2, half_b, recv3, total_b, gathered,
+    lengths_hbm, routes_hbm, frames, hidden, weight, taps_hbm, conv_grad,
+    out, gathered,
+    lengths, routes, frames_v, hidden_v, weight_v, taps_v, conv_v, out_v,
+    flags, glu, padded, taps_f, coef, phase, conv_back, dproj,
+    send1, recv1, piece, piece_b, recv2, half_b, recv3, total_b,
     load_sem, store_sem,
     send1_sem, recv1_sem, send2_sem, recv2_sem, send3_sem, recv3_sem, send4_sem, recv4_sem,
 ):
     node, local = lax.axis_index("node"), lax.axis_index("local")
     z, core = local // 2, local % 2
     partner = local + 1 - 2 * core
-
-    def loads():
-        yield frames, frames_v, 0
-        yield hidden.at[0], hidden_v, 1
-        yield taps_hbm, taps_v, 2
-        yield conv_grad, conv_v, 3
-        for cb in range(8):
-            for part in range(2):
-                yield (
-                    weight.at[:, pl.ds(part * 1024 + cb * TILE, TILE)],
-                    weight_v.at[:, pl.ds(cb * 256 + part * TILE, TILE)],
-                    4 + cb * 2 + part,
-                )
-
-    copies = [pltpu.make_async_copy(s, d, load_sem.at[i]) for s, d, i in loads()]
-    for copy in copies:
-        copy.start()
+    y, x = node // 4, node % 4
+
+    def load(source, target, i):
+        return pltpu.make_async_copy(source, target, load_sem.at[i])
+
+    def load_weight(cb, part):
+        start = pl.multiple_of(cb * TILE, TILE)
+        return load(
+            weight.at[:, pl.ds(part * 1024 + start, TILE)],
+            weight_v.at[:, pl.ds(pl.multiple_of(cb * 256, 256) + part * TILE, TILE)],
+            4 + cb * 2 + part,
+        )
+
+    load_frames = load(frames, frames_v, 0)
+    load_hidden = load(hidden.at[0], hidden_v, 1)
+    load_taps = load(taps_hbm, taps_v, 2)
+    load_conv = load(conv_grad, conv_v, 3)
+    load_lengths = load(lengths_hbm, lengths, 20)
+    load_routes = load(routes_hbm, routes, 21)
+    load_routes.start()
+    load_lengths.start()
+    load_frames.start()
+    load_hidden.start()
 
     barrier = pltpu.get_barrier_semaphore()
 
@@ -65,6 +72,8 @@
     lax.fori_loop(1, 8, greet_z, 0)
     pl.semaphore_signal(barrier, inc=1, device_id=(node, partner), device_id_type=MESH)
 
+    load_routes.wait()
+    load_lengths.wait()
     lane = lax.broadcasted_iota(I32, (1, TILE), 1)
     for r in range(8):
         named = routes[:, r * TILE:(r + 1) * TILE] == 0
@@ -86,7 +95,7 @@
     chosen = jnp.concatenate(
         [(jnp.broadcast_to(flags[r:r + 1, :], (32, TILE)) == want).astype(F32) for r in range(8)], axis=1
     ).astype(BF16)
-    copies[0].wait()
+    load_frames.wait()
     slot = jnp.dot(chosen, frames_v[...], preferred_element_type=F32)[0:CAPR]
 
     group = lax.broadcasted_iota(I32, (CAPR, TILE), 1) // 32
@@ -102,7 +111,7 @@
                     tile = part if tile is None else jnp.where(group == i, part, tile)
                 tiles.append(tile)
         sets.append(jnp.concatenate(tiles, axis=0).astype(BF16))
-    copies[1].wait()
+    load_hidden.wait()
     for m in range(8):
         columns = [
             hidden_v[:, (m * 4 + t) * TILE:(m * 4 + t + 1) * TILE].astype(F32) for t in range(4)
@@ -118,7 +127,7 @@
     rows1 = ((0, 144), (144, 48))
 
     def copy1(chunk, o):
-        to = (node + o) % 16
+        to = (y + o // 4) % 4 * 4 + (x + o % 4) % 4
         rows = pl.ds(*rows1[chunk])
         return pltpu.make_async_remote_copy(
             src_ref=send1.at[to, rows], dst_ref=recv1.at[node, rows],
@@ -142,13 +151,18 @@
         )
 
     def copy4(chunk, o):
-        to = (node + o) % 16
+        to = (y + o // 4) % 4 * 4 + (x + o % 4) % 4
         return pltpu.make_async_remote_copy(
             src_ref=total_b.at[chunk], dst_ref=gathered.at[node, pl.ds(2 * chunk, 2)],
             send_sem=send4_sem.at[chunk, o], recv_sem=recv4_sem.at[chunk, o],
             device_id=(to, local), device_id_type=MESH,
         )
 
+    def keep_own(chunk):
+        return pltpu.make_async_copy(
+            total_b.at[chunk], gathered.at[node, pl.ds(2 * chunk, 2)], load_sem.at[chunk]
+        )
+
     def each(count, do):
         def step(o, c):
             do(o)
@@ -156,8 +170,23 @@
 
         lax.fori_loop(1, count, step, 0)
 
-    for chunk in range(CHUNKS):
-        each(16, lambda o: copy1(chunk, o).start())
+    for o in FAR_FIRST:
+        copy1(0, o).start()
+    load_weight(0, 0).start()
+    load_weight(0, 1).start()
+    load_weight(1, 0).start()
+    load_weight(1, 1).start()
+    load_taps.start()
+    load_conv.start()
+    for cb in range(2, 8):
+        load_weight(cb, 0).start()
+        load_weight(cb, 1).start()
+
+
+    def send_rest():
+        each(16, lambda o: copy1(0, o).wait_send())
+        for o in FAR_FIRST:
+            copy1(1, o).start()
 
     def multiply(chunk):
         each(16, lambda o: copy1(chunk, o).wait_recv())
@@ -180,7 +209,8 @@
         half = piece[chunk, core] + recv2[chunk].astype(F32)
         half_b[chunk] = half.astype(BF16).reshape(8, 32, 256)
         recv3[chunk, z] = half_b[chunk, z]
-        each(8, lambda o: copy3(chunk, o).start())
+        for o in (4, 3, 5, 2, 6, 1, 7):
+            copy3(chunk, o).start()
 
     def add_chips(chunk):
         each(8, lambda o: copy3(chunk, o).wait_recv())
@@ -190,11 +220,12 @@
         total = total.astype(BF16)
         for t in range(2):
             total_b[chunk, t] = total[:, t * TILE:(t + 1) * TILE]
-        for t in range(2):
-            gathered[node, 2 * chunk + t] = total_b[chunk, t]
-        each(16, lambda o: copy4(chunk, o).start())
+        keep_own(chunk).start()
+        for o in FAR_FIRST:
+            copy4(chunk, o).start()
 
     steps = {
+        slots[6]: send_rest,
         slots[0]: lambda: multiply(0),
         slots[1]: lambda: multiply(1),
         slots[2]: lambda: add_cores(0),
@@ -208,53 +239,91 @@
             pl.when(now == at)(step)
 
     padded[0:16, :] = jnp.zeros((16, TILE), F32)
-    padded[272:288, :] = jnp.zeros((16, TILE), F32)
-    for copy in copies[2:]:
-        copy.wait()
+    padded[272:304, :] = jnp.zeros((32, TILE), F32)
+    taps_f[...] = jnp.zeros((40, TILE), F32)
+    load_taps.wait()
+    load_conv.wait()
     R = 64
-
-    def conv_tile(u, cb):
+    Q = UTT_LEN // 4
+
+    def coefficients(cb):
+        taps_f[1:KW + 1, :] = taps_v[:, pl.ds(pl.multiple_of(cb * TILE, TILE), TILE)].astype(F32)
+        u0, u1, u2, u3 = (taps_f[pl.ds(3 - m, 8, stride=4), :] for m in range(4))
+        filters = (u0 + u1 + u2 + u3, u0 + u1, u2 + u3, u0 + u2, u0, u2, u1 + u3, u1, u3)
+        for i, rows in enumerate(filters):
+            coef[i * 8:i * 8 + 8, :] = rows
+
+    def conv_tile(u, cb, at):
         rows_u = pl.multiple_of(u * UTT_LEN, UTT_LEN)
         lanes = pl.ds(pl.multiple_of(cb * TILE, TILE), TILE)
         valid = lax.broadcasted_iota(I32, (UTT_LEN, TILE), 0) < lengths[0, u]
         padded[16:272, :] = jnp.where(valid, conv_v[pl.ds(rows_u, UTT_LEN), lanes].astype(F32), 0.0)
-        taps = taps_v[:, lanes].astype(F32)
+        x0, x1, x2, x3, x4, x5, x6 = (padded[pl.ds(1 + m, Q + 8, stride=4), :] for m in range(7))
+        d0, d1, d2 = x0 - x1, x2 - x3, x4 - x5
+        e0, e1, e2 = x2 - x1, x4 - x3, x6 - x5
+        inputs = (x3, x1 - x3, x5 - x3, d1, d0 - d1, d2 - d1, e1, e0 - e1, e2 - e1)
+        for i, rows in enumerate(inputs):
+            phase[i] = rows
+
+        def correlate(i):
+            acc = None
+            for j in range(8):
+                term = coef[i * 8 + 7 - j:i * 8 + 8 - j, :] * phase[i, j:j + Q, :]
+                acc = term if acc is None else acc + term
+            return acc
+
+        q0, q1, q2 = correlate(0), correlate(1), correlate(2)
+        qa, qb = q0 + q1, q0 + q2
+        r0, r1, r2 = correlate(3), correlate(4), correlate(5)
+        conv_back[pl.ds(0, Q, stride=4), :] = qa + (r0 + r1)
+        conv_back[pl.ds(2, Q, stride=4), :] = qb + (r0 + r2)
+        t0, t1, t2 = correlate(6), correlate(7), correlate(8)
+        conv_back[pl.ds(1, Q, stride=4), :] = qa + (t0 + t1)
+        conv_back[pl.ds(3, Q, stride=4), :] = qb + (t0 + t2)
         for r in range(UTT_LEN // R):
             rows = pl.ds(pl.multiple_of(rows_u + r * R, R), R)
-            acc = jnp.zeros((R, TILE), F32)
-            for k in range(KW):
-                first = r * R + KW - k
-                acc = acc + taps[k:k + 1, :] * padded[first:first + R, :]
-            acc = jnp.where(valid[r * R:(r + 1) * R], acc, 0.0)
-            value, gate = glu[rows, 0:TILE], glu[rows, TILE:2 * TILE]
+            acc = jnp.where(valid[r * R:(r + 1) * R], conv_back[r * R:(r + 1) * R, :], 0.0)
+            value, gate = glu[rows, pl.ds(at, TILE)], glu[rows, pl.ds(at + TILE, TILE)]
             sig = jax.nn.sigmoid(gate)
             d_value = acc * sig
             d_gate = d_value * value * (1.0 - sig)
-            at = pl.multiple_of(cb * 256, 256)
-            dproj[rows, pl.ds(at, TILE)] = d_value.astype(BF16)
-            dproj[rows, pl.ds(at + TILE, TILE)] = d_gate.astype(BF16)
-
-    def channels(cb, c):
-        columns = pl.ds(pl.multiple_of(cb * 256, 256), 256)
+            to = pl.multiple_of(cb * 256, 256)
+            dproj[rows, pl.ds(to, TILE)] = d_value.astype(BF16)
+            dproj[rows, pl.ds(to + TILE, TILE)] = d_gate.astype(BF16)
+
+    def channels(pair, c):
+        columns = pl.ds(pl.multiple_of(pair * 512, 512), 512)
+        for t in range(2):
+            for part in range(2):
+                load_weight(pair * 2 + t, part).wait()
         glu[...] = jnp.dot(frames_v[...], weight_v[:, columns], preferred_element_type=F32)
 
-        def utterance(u, c):
-            conv_tile(u, cb)
-            hook(cb * 4 + u)
-            return c
-
-        return lax.fori_loop(0, 4, utterance, c)
-
-    lax.fori_loop(0, 8, channels, 0)
+        def one(t, c):
+            coefficients(pair * 2 + t)
+
+            def utterance(u, c):
+                conv_tile(u, pair * 2 + t, pl.multiple_of(t * 256, 256))
+                hook(pair * 8 + t * 4 + u)
+                return c
+
+            return lax.fori_loop(0, 4, utterance, c)
+
+        return lax.fori_loop(0, 2, one, c)
+
+    lax.fori_loop(0, 4, channels, 0)
+
+    def quarter(i):
+        rows = pl.ds(pl.multiple_of(i % 2 * 512, 512), 512)
+        return rows, pl.ds(pl.multiple_of(i // 2 * 512, 512), 512)
 
     def store(i):
-        columns = pl.ds(pl.multiple_of(i * 256, 256), 256)
-        return pltpu.make_async_copy(out_v.at[:, columns], out.at[:, columns], store_sem.at[i])
+        part = quarter(i)
+        return pltpu.make_async_copy(out_v.at[*part], out.at[*part], store_sem.at[i])
 
     def back(i, c):
-        columns = pl.ds(pl.multiple_of(i * 256, 256), 256)
-        out_v[:, columns] = lax.dot_general(
-            dproj[...], weight_v[columns, :], (((1,), (1,)), ((), ())), preferred_element_type=F32
+        rows, columns = quarter(i)
+        out_v[rows, columns] = lax.dot_general(
+            dproj[rows, :], weight_v[columns, :], (((1,), (1,)), ((), ())), preferred_element_type=F32
         ).astype(BF16)
         store(i).start()
         hook(32 + i)
@@ -262,60 +331,97 @@
 
     lax.fori_loop(0, 4, back, 0)
 
+    for chunk in range(CHUNKS):
+        each(16, lambda o: copy4(chunk, o).wait_recv())
+    for chunk in range(CHUNKS):
+        if chunk:
+            each(16, lambda o: copy1(chunk, o).wait_send())
+        copy2(chunk).wait_send()
+        each(8, lambda o: copy3(chunk, o).wait_send())
+        each(16, lambda o: copy4(chunk, o).wait_send())
+    for i in range(4):
+        store(i).wait()
+    for chunk in range(CHUNKS):
+        keep_own(chunk).wait()
+
+
+def finish(owners_hbm, grad, gathered, out, owned, owners, through, blocks, owned_v, owners_sem, move_sem, block_sem, owned_sem):
+    node = lax.axis_index("node")
+
+    def move_in(i):
+        rows = pl.ds(i * 256, 256)
+        return pltpu.make_async_copy(grad.at[rows], through.at[rows], move_sem.at[0, i])
+
+    def move_out(i):
+        rows = pl.ds(i * 256, 256)
+        return pltpu.make_async_copy(through.at[rows], out.at[rows], move_sem.at[1, i])
+
+    load_owners = pltpu.make_async_copy(owners_hbm, owners, owners_sem)
+    load_owners.start()
+    for i in range(4):
+        move_in(i).start()
+    load_owners.wait()
     picks = [jnp.int32(-1)] * CAP
     held = jnp.int32(0)
     for i in range(32):
         mine = owners[i] == node
         picks = [jnp.where(mine & (held == k), i, picks[k]) for k in range(CAP)]
         held = held + mine.astype(I32)
-    for chunk in range(CHUNKS):
-        each(16, lambda o: copy4(chunk, o).wait_recv())
+
+    def fetch(k, g):
+        block = jnp.maximum(picks[k], 0)
+        return pltpu.make_async_copy(
+            gathered.at[g * 8 + block // 4, block % 4], blocks.at[k, g], block_sem.at[k, g]
+        )
+
     for k in range(CAP):
-        block = jnp.maximum(picks[k], 0)
+        for g in range(2):
+            fetch(k, g).start()
+    for i in range(4):
+        move_in(i).wait()
+        move_out(i).start()
+    for k in range(CAP):
         keep = jnp.broadcast_to(picks[k] >= 0, (32, TILE))
         for g in range(2):
-            rows = gathered[g * 8 + block // 4, block % 4].astype(F32)
-            owned_v[k, g * 32:(g + 1) * 32, :] = jnp.where(keep, rows, 0.0)
-    last = pltpu.make_async_copy(owned_v, owned, load_sem.at[0])
+            fetch(k, g).wait()
+            owned_v[k, g * 32:(g + 1) * 32, :] = jnp.where(keep, blocks[k, g].astype(F32), 0.0)
+    last = pltpu.make_async_copy(owned_v, owned, owned_sem)
     last.start()
-
-    for chunk in range(CHUNKS):
-        each(16, lambda o: copy1(chunk, o).wait_send())
-        copy2(chunk).wait_send()
-        each(8, lambda o: copy3(chunk, o).wait_send())
-        each(16, lambda o: copy4(chunk, o).wait_send())
     for i in range(4):
-        store(i).wait()
+        move_out(i).wait()
     last.wait()
 
 
-SLOTS = (13, 17, 16, 20, 23, 28)
+SLOTS = (16, 22, 19, 26, 29, 33, 13)
 
 
 def shards(frames, lengths, routes, owners, pw_weight, dw_kernel, conv_grad, hidden_grad):
-    smem = pl.BlockSpec(memory_space=pltpu.SMEM)
-    vmem = pl.BlockSpec(memory_space=pltpu.VMEM)
     hbm = pl.BlockSpec(memory_space=pl.ANY)
     dma = pltpu.SemaphoreType.DMA
-    return pl.pallas_call(
+    grad, gathered = pl.pallas_call(
         functools.partial(kernel, SLOTS),
         out_shape=(
             jax.ShapeDtypeStruct((1024, 1024), BF16),
-            jax.ShapeDtypeStruct((CAP, 64, TILE), F32),
+            jax.ShapeDtypeStruct((16, 4, 32, TILE), BF16),
         ),
-        in_specs=[smem, smem, vmem, hbm, hbm, hbm, hbm, hbm],
+        in_specs=[hbm] * 7,
         out_specs=(hbm, hbm),
         scratch_shapes=[
+            pltpu.SMEM((1, 4), I32),
+            pltpu.VMEM((2, 1024), I32),
             pltpu.VMEM((1024, 1024), BF16),
             pltpu.VMEM((CAPR, 4096), BF16),
             pltpu.VMEM((1024, 2048), BF16),
             pltpu.VMEM((KW, 1024), BF16),
             pltpu.VMEM((1024, 1024), BF16),
             pltpu.VMEM((1024, 1024), BF16),
-            pltpu.VMEM((CAP, 64, TILE), F32),
             pltpu.VMEM((8, TILE), F32),
-            pltpu.VMEM((1024, 256), F32),
-            pltpu.VMEM((288, TILE), F32),
+            pltpu.VMEM((1024, 512), F32),
+            pltpu.VMEM((304, TILE), F32),
+            pltpu.VMEM((40, TILE), F32),
+            pltpu.VMEM((72, TILE), F32),
+            pltpu.VMEM((9, 72, TILE), F32),
+            pltpu.VMEM((256, TILE), F32),
             pltpu.VMEM((1024, 2048), BF16),
             pltpu.VMEM((16, 192, TILE), BF16),
             pltpu.VMEM((16, 192, TILE), BF16),
@@ -325,8 +431,7 @@
             pltpu.VMEM((CHUNKS, 8, 32, 256), BF16),
             pltpu.VMEM((CHUNKS, 8, 32, 256), BF16),
             pltpu.VMEM((CHUNKS, 2, 32, TILE), BF16),
-            pltpu.VMEM((16, 4, 32, TILE), BF16),
-            dma((20,)), dma((4,)),
+            dma((22,)), dma((4,)),
             dma((CHUNKS, 16)), dma((CHUNKS, 16)),
             dma((CHUNKS,)), dma((CHUNKS,)),
             dma((CHUNKS, 8)), dma((CHUNKS, 8)),
@@ -336,8 +441,25 @@
             collective_id=0, has_side_effects=True, vmem_limit_bytes=56 * 2**20
         ),
     )(
-        lengths, owners.reshape(32), routes.T, frames, hidden_grad, pw_weight, dw_kernel, conv_grad
+        lengths, routes.T, frames, hidden_grad, pw_weight, dw_kernel, conv_grad
     )
+    return pl.pallas_call(
+        finish,
+        out_shape=(
+            jax.ShapeDtypeStruct((1024, 1024), BF16),
+            jax.ShapeDtypeStruct((CAP, 64, TILE), F32),
+        ),
+        in_specs=[hbm] * 3,
+        out_specs=(hbm, hbm),
+        scratch_shapes=[
+            pltpu.SMEM((32,), I32),
+            pltpu.VMEM((1024, 1024), BF16),
+            pltpu.VMEM((CAP, 2, 32, TILE), BF16),
+            pltpu.VMEM((CAP, 64, TILE), F32),
+            dma, dma((2, 4)), dma((CAP, 2)), dma,
+        ],
+        compiler_params=pltpu.CompilerParams(vmem_limit_bytes=56 * 2**20),
+    )(owners.reshape(32), grad, gathered)
 
 
 def solution(mesh):

time: 45.7 us -> 42.9 us (0.939)
  the two profiles are of different devices: /device:TPU:4 before, /device:TPU:32 now
where the time goes in v2:
time: 42.9 us; the launch traced here: 42.4 us
  Pallas kernels  41.7 us (97%)
  between operations  0.64 us (1%)
    pallas_call x1, Pallas kernels, shards(): pl.pallas_call(functools.partial(kernel, SLOTS), out_shape=(jax.ShapeDtyp...  38.8 us
    pallas_call x1, Pallas kernels, shards(): pl.pallas_call(finish, out_shape=(jax.ShapeDtypeStruct((1024, 1024), BF16...  2.93 us

profile of v2, /device:TPU:32, one launch (start us, length us, event | category | flops | bytes accessed | tf_op | source)
XLA Modules:
  0.0 42.4 jit_solution(4823113842815010725)
XLA Ops:
  0.6 38.8 %shard_map.95 = (bf16[1024,1024]{1,0:T(8,128)(2,1)}, bf16[16,4,32,128]{3,2,1,0:T(8,128)(2,1)}) custom-call(s32[1,4]{1,0:T(1,128)} %lengths_hbm.1, s32[2,1024]{1,0:T(2,128)} %bitcast.2, bf16[1024,1024]{1,0:T(8,128)(2,1)} %frames.1, bf16[1,24,4096]{2,1,0:T(8,128)(2,1)} %hidden.1, bf16[1024,2048]{1,0:T(8,128)(2,1)} %weight.1, bf16[31,1024]{1,0:T(8,128)(2,1)} %taps_hbm.1, ...), custom_call_target="tpu_custom_call" | custom-call | tf_op jit(solution)/shard_map/pallas_call | solution.py:401
  39.4 2.9 %shard_map.96 = (bf16[1024,1024]{1,0:T(8,128)(2,1)}, f32[6,64,128]{2,1,0:T(8,128)}) custom-call(s32[32]{0:T(128)} %bitcast.3, bf16[1024,1024]{1,0:T(8,128)(2,1)} %get-tuple-element.4.grad, bf16[16,4,32,128]{3,2,1,0:T(8,128)(2,1)} %get-tuple-element.5.gathered), custom_call_target="tpu_custom_call" | custom-call | tf_op jit(solution)/shard_map/pallas_call | solution.py:446

commit v3 on v2

--- a/solution.py
+++ b/solution.py
@@ -55,6 +55,12 @@
     load_lengths.start()
     load_frames.start()
     load_hidden.start()
+    load_weight(0, 0).start()
+    load_weight(0, 1).start()
+    load_weight(1, 0).start()
+    load_weight(1, 1).start()
+    load_taps.start()
+    load_conv.start()
 
     barrier = pltpu.get_barrier_semaphore()
 
@@ -172,12 +178,6 @@
 
     for o in FAR_FIRST:
         copy1(0, o).start()
-    load_weight(0, 0).start()
-    load_weight(0, 1).start()
-    load_weight(1, 0).start()
-    load_weight(1, 1).start()
-    load_taps.start()
-    load_conv.start()
     for cb in range(2, 8):
         load_weight(cb, 0).start()
         load_weight(cb, 1).start()

time: 42.9 us -> 41 us (0.956)
  Pallas kernels: 41.7 us -> 40.2 us
    pallas_call x1, Pallas kernels: 38.8 us -> 37.2 us  [shards(): pl.pallas_call(functools.partial(kernel, SLOTS), out_shape=(jax.ShapeDtyp...]
where the time goes in v3:
time: 41 us; the launch traced here: 40.8 us
  Pallas kernels  40.2 us (98%)
  between operations  0.64 us (2%)
    pallas_call x1, Pallas kernels, shards(): pl.pallas_call(functools.partial(kernel, SLOTS), out_shape=(jax.ShapeDtyp...  37.2 us
    pallas_call x1, Pallas kernels, shards(): pl.pallas_call(finish, out_shape=(jax.ShapeDtypeStruct((1024, 1024), BF16...  2.93 us

profile of v3, /device:TPU:32, one launch (start us, length us, event | category | flops | bytes accessed | tf_op | source)
XLA Modules:
  0.0 40.8 jit_solution(17354339232306748835)
XLA Ops:
  0.6 37.2 %shard_map.95 = (bf16[1024,1024]{1,0:T(8,128)(2,1)}, bf16[16,4,32,128]{3,2,1,0:T(8,128)(2,1)}) custom-call(s32[1,4]{1,0:T(1,128)} %lengths_hbm.1, s32[2,1024]{1,0:T(2,128)} %bitcast.2, bf16[1024,1024]{1,0:T(8,128)(2,1)} %frames.1, bf16[1,24,4096]{2,1,0:T(8,128)(2,1)} %hidden.1, bf16[1024,2048]{1,0:T(8,128)(2,1)} %weight.1, bf16[31,1024]{1,0:T(8,128)(2,1)} %taps_hbm.1, ...), custom_call_target="tpu_custom_call" | custom-call | tf_op jit(solution)/shard_map/pallas_call | solution.py:401
  37.9 2.9 %shard_map.96 = (bf16[1024,1024]{1,0:T(8,128)(2,1)}, f32[6,64,128]{2,1,0:T(8,128)}) custom-call(s32[32]{0:T(128)} %bitcast.3, bf16[1024,1024]{1,0:T(8,128)(2,1)} %get-tuple-element.4.grad, bf16[16,4,32,128]{3,2,1,0:T(8,128)(2,1)} %get-tuple-element.5.gathered), custom_call_target="tpu_custom_call" | custom-call | tf_op jit(solution)/shard_map/pallas_call | solution.py:446

commit v4 on v3

--- a/solution.py
+++ b/solution.py
@@ -25,7 +25,7 @@
     out, gathered,
     lengths, routes, frames_v, hidden_v, weight_v, taps_v, conv_v, out_v,
     flags, glu, padded, taps_f, coef, phase, conv_back, dproj,
-    send1, recv1, piece, piece_b, recv2, half_b, recv3, total_b,
+    send1, recv1, left_t, piece, piece_b, recv2, half_b, recv3, total_b,
     load_sem, store_sem,
     send1_sem, recv1_sem, send2_sem, recv2_sem, send3_sem, recv3_sem, send4_sem, recv4_sem,
 ):
@@ -197,8 +197,9 @@
             parts = [rows[:, t].reshape(16 * CAPR, TILE) for t in range(count)]
             return jnp.concatenate(parts, axis=1).astype(BF16)
 
-        left, right = tiles(0, 4), tiles(4 + 2 * chunk, 2)
-        both = lax.dot_general(left, right, (((0,), (0,)), ((), ())), preferred_element_type=F32)
+        if chunk == 0:
+            left_t[...] = tiles(0, 4).T
+        both = jnp.dot(left_t[...], tiles(4 + 2 * chunk, 2), preferred_element_type=F32)
         both = both.reshape(2, 256, 256)
         piece[chunk] = both
         piece_b[chunk] = both.astype(BF16)
@@ -220,9 +221,9 @@
         total = total.astype(BF16)
         for t in range(2):
             total_b[chunk, t] = total[:, t * TILE:(t + 1) * TILE]
-        keep_own(chunk).start()
         for o in FAR_FIRST:
             copy4(chunk, o).start()
+        keep_own(chunk).start()
 
     steps = {
         slots[6]: send_rest,
@@ -331,21 +332,20 @@
 
     lax.fori_loop(0, 4, back, 0)
 
+    each(16, lambda o: copy1(1, o).wait_send())
     for chunk in range(CHUNKS):
-        each(16, lambda o: copy4(chunk, o).wait_recv())
-    for chunk in range(CHUNKS):
-        if chunk:
-            each(16, lambda o: copy1(chunk, o).wait_send())
         copy2(chunk).wait_send()
         each(8, lambda o: copy3(chunk, o).wait_send())
-        each(16, lambda o: copy4(chunk, o).wait_send())
+        keep_own(chunk).wait()
     for i in range(4):
         store(i).wait()
     for chunk in range(CHUNKS):
-        keep_own(chunk).wait()
-
-
-def finish(owners_hbm, grad, gathered, out, owned, owners, through, blocks, owned_v, owners_sem, move_sem, block_sem, owned_sem):
+        each(16, lambda o: copy4(chunk, o).wait_send())
+    for chunk in range(CHUNKS):
+        each(16, lambda o: copy4(chunk, o).wait_recv())
+
+
+def finish(owners_hbm, grad, gathered, out, owned, owners, picks, through, blocks, owned_v, owners_sem, move_sem, block_sem, owned_sem):
     node = lax.axis_index("node")
 
     def move_in(i):
@@ -361,15 +361,13 @@
     for i in range(4):
         move_in(i).start()
     load_owners.wait()
-    picks = [jnp.int32(-1)] * CAP
     held = jnp.int32(0)
     for i in range(32):
-        mine = owners[i] == node
-        picks = [jnp.where(mine & (held == k), i, picks[k]) for k in range(CAP)]
-        held = held + mine.astype(I32)
+        picks[held] = jnp.int32(i)
+        held = held + (owners[i] == node).astype(I32)
 
     def fetch(k, g):
-        block = jnp.maximum(picks[k], 0)
+        block = jnp.where(k < held, picks[k], 0)
         return pltpu.make_async_copy(
             gathered.at[g * 8 + block // 4, block % 4], blocks.at[k, g], block_sem.at[k, g]
         )
@@ -381,7 +379,7 @@
         move_in(i).wait()
         move_out(i).start()
     for k in range(CAP):
-        keep = jnp.broadcast_to(picks[k] >= 0, (32, TILE))
+        keep = jnp.broadcast_to(k < held, (32, TILE))
         for g in range(2):
             fetch(k, g).wait()
             owned_v[k, g * 32:(g + 1) * 32, :] = jnp.where(keep, blocks[k, g].astype(F32), 0.0)
@@ -425,6 +423,7 @@
             pltpu.VMEM((1024, 2048), BF16),
             pltpu.VMEM((16, 192, TILE), BF16),
             pltpu.VMEM((16, 192, TILE), BF16),
+            pltpu.VMEM((512, 16 * CAPR), BF16),
             pltpu.VMEM((CHUNKS, 2, 256, 256), F32),
             pltpu.VMEM((CHUNKS, 2, 256, 256), BF16),
             pltpu.VMEM((CHUNKS, 256, 256), BF16),
@@ -453,6 +452,7 @@
         out_specs=(hbm, hbm),
         scratch_shapes=[
             pltpu.SMEM((32,), I32),
+            pltpu.SMEM((33,), I32),
             pltpu.VMEM((1024, 1024), BF16),
             pltpu.VMEM((CAP, 2, 32, TILE), BF16),
             pltpu.VMEM((CAP, 64, TILE), F32),

time: 41 us -> 40.3 us (0.983)
  Pallas kernels: 40.2 us -> 39.6 us
    pallas_call x1, Pallas kernels: 37.2 us -> 36.8 us  [shards(): pl.pallas_call(functools.partial(kernel, SLOTS), out_shape=(jax.ShapeDtyp...]
where the time goes in v4:
time: 40.3 us; the launch traced here: 40.2 us
  Pallas kernels  39.6 us (98%)
  between operations  0.64 us (2%)
    pallas_call x1, Pallas kernels, shards(): pl.pallas_call(functools.partial(kernel, SLOTS), out_shape=(jax.ShapeDtyp...  36.8 us
    pallas_call x1, Pallas kernels, shards(): pl.pallas_call(finish, out_shape=(jax.ShapeDtypeStruct((1024, 1024), BF16...  2.76 us

profile of v4, /device:TPU:32, one launch (start us, length us, event | category | flops | bytes accessed | tf_op | source)
XLA Modules:
  0.0 40.2 jit_solution(11991439088451929397)
XLA Ops:
  0.6 36.8 %shard_map.95 = (bf16[1024,1024]{1,0:T(8,128)(2,1)}, bf16[16,4,32,128]{3,2,1,0:T(8,128)(2,1)}) custom-call(s32[1,4]{1,0:T(1,128)} %lengths_hbm.1, s32[2,1024]{1,0:T(2,128)} %bitcast.2, bf16[1024,1024]{1,0:T(8,128)(2,1)} %frames.1, bf16[1,24,4096]{2,1,0:T(8,128)(2,1)} %hidden.1, bf16[1024,2048]{1,0:T(8,128)(2,1)} %weight.1, bf16[31,1024]{1,0:T(8,128)(2,1)} %taps_hbm.1, ...), custom_call_target="tpu_custom_call" | custom-call | tf_op jit(solution)/shard_map/pallas_call | solution.py:399
  37.4 2.8 %shard_map.96 = (bf16[1024,1024]{1,0:T(8,128)(2,1)}, f32[6,64,128]{2,1,0:T(8,128)}) custom-call(s32[32]{0:T(128)} %bitcast.3, bf16[1024,1024]{1,0:T(8,128)(2,1)} %get-tuple-element.4.grad, bf16[16,4,32,128]{3,2,1,0:T(8,128)(2,1)} %get-tuple-element.5.gathered), custom_call_target="tpu_custom_call" | custom-call | tf_op jit(solution)/shard_map/pallas_call | solution.py:445

commit v5 on v4

--- a/solution.py
+++ b/solution.py
@@ -34,6 +34,22 @@
     partner = local + 1 - 2 * core
     y, x = node // 4, node % 4
 
+    barrier = pltpu.get_barrier_semaphore()
+
+    def greet(o, c):
+        pl.semaphore_signal(barrier, inc=1, device_id=((node + o) % 16, local), device_id_type=MESH)
+        return c
+
+    def greet_z(o, c):
+        pl.semaphore_signal(
+            barrier, inc=1, device_id=(node, (z + o) % 8 * 2 + core), device_id_type=MESH
+        )
+        return c
+
+    lax.fori_loop(1, 16, greet, 0)
+    lax.fori_loop(1, 8, greet_z, 0)
+    pl.semaphore_signal(barrier, inc=1, device_id=(node, partner), device_id_type=MESH)
+
     def load(source, target, i):
         return pltpu.make_async_copy(source, target, load_sem.at[i])
 
@@ -45,7 +61,9 @@
             4 + cb * 2 + part,
         )
 
-    load_frames = load(frames, frames_v, 0)
+    load_frames = [
+        load(frames.at[pl.ds(i * 256, 256)], frames_v.at[pl.ds(i * 256, 256)], 22 + i) for i in range(4)
+    ]
     load_hidden = load(hidden.at[0], hidden_v, 1)
     load_taps = load(taps_hbm, taps_v, 2)
     load_conv = load(conv_grad, conv_v, 3)
@@ -53,7 +71,8 @@
     load_routes = load(routes_hbm, routes, 21)
     load_routes.start()
     load_lengths.start()
-    load_frames.start()
+    for part in load_frames:
+        part.start()
     load_hidden.start()
     load_weight(0, 0).start()
     load_weight(0, 1).start()
@@ -61,22 +80,6 @@
     load_weight(1, 1).start()
     load_taps.start()
     load_conv.start()
-
-    barrier = pltpu.get_barrier_semaphore()
-
-    def greet(o, c):
-        pl.semaphore_signal(barrier, inc=1, device_id=((node + o) % 16, local), device_id_type=MESH)
-        return c
-
-    def greet_z(o, c):
-        pl.semaphore_signal(
-            barrier, inc=1, device_id=(node, (z + o) % 8 * 2 + core), device_id_type=MESH
-        )
-        return c
-
-    lax.fori_loop(1, 16, greet, 0)
-    lax.fori_loop(1, 8, greet_z, 0)
-    pl.semaphore_signal(barrier, inc=1, device_id=(node, partner), device_id_type=MESH)
 
     load_routes.wait()
     load_lengths.wait()
@@ -101,8 +104,12 @@
     chosen = jnp.concatenate(
         [(jnp.broadcast_to(flags[r:r + 1, :], (32, TILE)) == want).astype(F32) for r in range(8)], axis=1
     ).astype(BF16)
-    load_frames.wait()
-    slot = jnp.dot(chosen, frames_v[...], preferred_element_type=F32)[0:CAPR]
+    slot = jnp.zeros((32, 1024), F32)
+    for i in range(4):
+        load_frames[i].wait()
+        part = pl.ds(i * 256, 256)
+        slot = slot + jnp.dot(chosen[:, i * 256:(i + 1) * 256], frames_v[part, :], preferred_element_type=F32)
+    slot = slot[0:CAPR]
 
     group = lax.broadcasted_iota(I32, (CAPR, TILE), 1) // 32
     sets = []
@@ -390,7 +397,7 @@
     last.wait()
 
 
-SLOTS = (16, 22, 19, 26, 29, 33, 13)
+SLOTS = (15, 21, 18, 25, 28, 32, 12)
 
 
 def shards(frames, lengths, routes, owners, pw_weight, dw_kernel, conv_grad, hidden_grad):
@@ -430,7 +437,7 @@
             pltpu.VMEM((CHUNKS, 8, 32, 256), BF16),
             pltpu.VMEM((CHUNKS, 8, 32, 256), BF16),
             pltpu.VMEM((CHUNKS, 2, 32, TILE), BF16),
-            dma((22,)), dma((4,)),
+            dma((26,)), dma((4,)),
             dma((CHUNKS, 16)), dma((CHUNKS, 16)),
             dma((CHUNKS,)), dma((CHUNKS,)),
             dma((CHUNKS, 8)), dma((CHUNKS, 8)),

time: 40.3 us -> 40.3 us (level); the launches traced: 40.2 us -> 39.6 us
  Pallas kernels: 39.6 us -> 39 us
    pallas_call x1, Pallas kernels: 36.8 us -> 36.2 us  [shards(): pl.pallas_call(functools.partial(kernel, SLOTS), out_shape=(jax.ShapeDtyp...]
where the time goes in v5:
time: 40.3 us; the launch traced here: 39.6 us
  Pallas kernels  39 us (97%)
  between operations  0.64 us (2%)
    pallas_call x1, Pallas kernels, shards(): pl.pallas_call(functools.partial(kernel, SLOTS), out_shape=(jax.ShapeDtyp...  36.2 us
    pallas_call x1, Pallas kernels, shards(): pl.pallas_call(finish, out_shape=(jax.ShapeDtypeStruct((1024, 1024), BF16...  2.76 us

profile of v5, /device:TPU:32, one launch (start us, length us, event | category | flops | bytes accessed | tf_op | source)
XLA Modules:
  0.0 39.6 jit_solution(9007534674287023470)
XLA Ops:
  0.6 36.2 %shard_map.95 = (bf16[1024,1024]{1,0:T(8,128)(2,1)}, bf16[16,4,32,128]{3,2,1,0:T(8,128)(2,1)}) custom-call(s32[1,4]{1,0:T(1,128)} %lengths_hbm.1, s32[2,1024]{1,0:T(2,128)} %bitcast.2, bf16[1024,1024]{1,0:T(8,128)(2,1)} %frames.1, bf16[1,24,4096]{2,1,0:T(8,128)(2,1)} %hidden.1, bf16[1024,2048]{1,0:T(8,128)(2,1)} %weight.1, bf16[31,1024]{1,0:T(8,128)(2,1)} %taps_hbm.1, ...), custom_call_target="tpu_custom_call" | custom-call | tf_op jit(solution)/shard_map/pallas_call | solution.py:406
  36.9 2.8 %shard_map.96 = (bf16[1024,1024]{1,0:T(8,128)(2,1)}, f32[6,64,128]{2,1,0:T(8,128)}) custom-call(s32[32]{0:T(128)} %bitcast.3, bf16[1024,1024]{1,0:T(8,128)(2,1)} %get-tuple-element.4.grad, bf16[16,4,32,128]{3,2,1,0:T(8,128)(2,1)} %get-tuple-element.5.gathered), custom_call_target="tpu_custom_call" | custom-call | tf_op jit(solution)/shard_map/pallas_call | solution.py:452
